TPU v7x, 128 devices: a whole 4x4x4 slice. The times are simulated.
128 devices in a mesh: dap: 64 (over y_lo, x, z, core), rep: 2 (over y_hi).
Axes of the slice: x: 4, y: 4 (y_hi: 2, y_lo: 2; y = y_hi * 2 + y_lo), z: 4, core: 2. Of those that a mesh axis runs over, the one named last changes fastest.
Arguments:
- pair_map: bfloat16 [1024, 1024, 128], P('dap'), may hold values from -6 to 6
- residue_mask: int32 [1024], replicated, may hold values from 0 to 1, as said below
- gain_start: float32 [128], replicated, may hold values from 0.25 to 1.75
- proj_start: bfloat16 [4, 128, 128], P(None, None, 'rep'), may hold values from -4 to 4
- bias_start: bfloat16 [128, 4], P(None, 'rep'), may hold values from -0.5 to 0.5
- out_start: bfloat16 [128, 128], replicated, may hold values from -3 to 3
- gain_end: float32 [128], replicated, may hold values from 0.25 to 1.75
- proj_end: bfloat16 [4, 128, 128], P(None, None, 'rep'), may hold values from -4 to 4
- bias_end: bfloat16 [128, 4], P(None, 'rep'), may hold values from -0.5 to 0.5
- out_end: bfloat16 [128, 128], replicated, may hold values from -3 to 3
Outputs:
- turned_map: bfloat16 [1024, 1024, 128], P('dap')
Inputs may be any that keep to these rules, and one draw needn't show every extreme that they name: residue_mask is 1 on the first L residues and 0 on the others, for some L from 512 to 1023.
All inputs are finite; a program needn't handle non-finite values.
Results may differ from a plain program's by a relative error of at most 0.008.
The roundings to bfloat16 on the way count: a program that leaves them out, or rounds other values in their place, can miss the bound.
Values may be sent and summed in bfloat16 or wider, within the bound.
A program may use at most 128 MiB of HBM per device.

v0:
```python
import functools
import math

import jax
import jax.numpy as jnp
from jax import lax
from jax.experimental import pallas as pl
from jax.experimental.pallas import tpu as pltpu
from jax.sharding import PartitionSpec as P

EPS = 1e-5
LOG2E = math.log2(math.e)
HEADS = 4
DH = 32
W = HEADS * DH
VMEM_LIMIT = 60 * 2**20
RING = 4
CORES = 2
MESH = pl.DeviceIdType.MESH


def place():
    dap, rep = lax.axis_index("dap"), lax.axis_index("rep")
    core = lax.rem(dap, CORES)
    z = lax.rem(dap // CORES, RING)
    x = lax.rem(dap // (CORES * RING), RING)
    y = rep * 2 + dap // (CORES * RING * RING)
    return {"c": core, "y": y, "x": x, "z": z}


def block_of(at):
    dap = ((lax.rem(at["y"], 2) * RING + at["x"]) * RING + at["z"]) * CORES + at["c"]
    return dap * 2 + at["y"] // 2


def device_of(at):
    dap = ((lax.rem(at["y"], 2) * RING + at["x"]) * RING + at["z"]) * CORES + at["c"]
    return {"dap": dap, "rep": at["y"] // 2}


def shifted(at, axis, by):
    size = CORES if axis == "c" else RING
    return {**at, axis: lax.rem(at[axis] + by + size, size)}


def normalize(floats, gain):
    center = jnp.mean(floats, axis=-1, keepdims=True)
    apart = floats - center
    spread = jnp.mean(apart * apart, axis=-1, keepdims=True)
    return (apart * lax.rsqrt(spread + EPS) * gain).astype(jnp.bfloat16)


ORDERS = ("xyz", "yzx", "zxy")
GRAIN = 32


def gather_parts(n):
    unit = n // 8
    return ((0, 3 * unit), (3 * unit, 3 * unit), (6 * unit, 2 * unit))


def module_kernel(*refs, first_module, n, rows):
    if first_module:
        (map_ref, mask_ref, gain_ref, half_ref, strip_ref, outw_ref, out_ref, w_out, bw_out) = refs[:9]
        (gat_ref, bias_ref, norm_ref, q_ref, k_ref, v_ref, g_ref, va_ref, score_ref, expo_ref, total_ref, base_ref,
         own32, stage_ref, core_send, core_recv, send, recv, local_sem, row_send, row_recv, row_local,
         done_ref, mail_ref, far_send, far_recv, far_local, w_ref, strip_in, w_send, w_recv) = refs[9:]
    else:
        (map_ref, mask_ref, gain_ref, w_ref, bw_ref, outw_ref, out_ref) = refs[:7]
        (gat_ref, bias_ref, norm_ref, q_ref, k_ref, v_ref, g_ref, va_ref, score_ref, expo_ref, total_ref, base_ref,
         own32, stage_ref, core_send, core_recv, send, recv, local_sem, row_send, row_recv, row_local) = refs[7:]
    me = place()
    rep = lax.axis_index("rep")
    peer = shifted(me, "y", 2)
    row0 = block_of(me) * rows
    steps = rows // 2
    span = n // 2
    column = [{**me, "y": lax.rem(me["y"] + k // CORES, RING), "c": lax.rem(me["c"] + k % CORES, CORES)}
              for k in range(CORES * RING)]
    level = [{**me, "x": lax.rem(me["x"] + k // RING, RING), "z": lax.rem(me["z"] + k % RING, RING)}
             for k in range(RING * RING)]
    lane = lax.broadcasted_iota(jnp.int32, (1, W), 1) // DH
    mask = mask_ref[...].astype(jnp.float32)
    length = jnp.sum(mask, axis=1, keepdims=True)
    valid = mask > 0.5

    if first_module:
        partners = column[1:] + level[1:]
    else:
        partners = [shifted(me, axis, by) for axis in "xyz" for by in (1, -1)] + [shifted(me, "c", 1), peer]
    barrier = pltpu.get_barrier_semaphore()
    for partner in partners:
        pl.semaphore_signal(barrier, inc=1, device_id=device_of(partner), device_id_type=MESH)

    started = []

    def push(src, dst, to, semaphores, number):
        copy = pltpu.make_async_remote_copy(
            src_ref=src, dst_ref=dst, send_sem=semaphores[0].at[number], recv_sem=semaphores[1].at[number],
            device_id=device_of(to), device_id_type=MESH,
        )
        copy.start()
        started.append(copy)
        return copy

    if first_module:
        fetch = pltpu.make_async_copy(map_ref.at[pl.ds(rep * rows, rows)], base_ref, local_sem.at[0])
        fetch.start()
        place_w = w_ref.at[:, :, pl.ds(rep * (W // 2), W // 2), :]
        keep_w = pltpu.make_async_copy(half_ref, place_w, local_sem.at[1])
        keep_w.start()
        pl.semaphore_wait(barrier, len(partners))
        strip_copy = push(strip_ref, strip_in, peer, (w_send, w_recv), 0)
        w_copy = push(half_ref, place_w, peer, (w_send, w_recv), 1)
        fetch.wait()
    else:
        four = 4 * rows * rows
        to = lax.broadcasted_iota(jnp.int32, (four, four), 0)
        come = lax.broadcasted_iota(jnp.int32, (four, four), 1)
        j, which, i = to // (4 * rows), (to // rows) % 4, to % rows
        turn = (come == ((i // 2 * 4 + which) * 2 + i % 2) * rows + j).astype(jnp.bfloat16)
        for low in range(2):
            for xz in range(RING * RING):
                piece = map_ref[:, xz, 4 * low:4 * low + 4].reshape(four, -1)
                result = jnp.dot(turn, piece, preferred_element_type=jnp.float32)
                first = (low * RING * RING + xz) * 4 * rows
                base_ref[:, first:first + 4 * rows, :] = result.reshape(rows, 4 * rows, -1).astype(jnp.bfloat16)

    def norm_row(i, carry):
        norm_ref[i] = normalize(base_ref[i].astype(jnp.float32), gain_ref[...])
        return carry

    lax.fori_loop(0, rows, norm_row, 0)
    if first_module:
        strip_copy.wait_recv()
        weights = strip_ref[0] + strip_in[0]
        later = strip_ref[1] + strip_in[1]
        bw_out[...] = later
    else:
        weights = bw_ref[...]

    def plane_row(i, carry):
        strip = lax.dot_general(weights, norm_ref[i], (((1,), (1,)), ((), ())), preferred_element_type=jnp.float32)
        for h in range(HEADS):
            own32[pl.ds(h * rows + i, 1), :] = strip[h:h + 1]
        return carry

    lax.fori_loop(0, rows, plane_row, 0)
    gat_ref[me["c"], me["y"], me["x"], me["z"]] = own32[...].astype(jnp.bfloat16)
    if not first_module:
        pl.semaphore_wait(barrier, len(partners))

    def project(i):
        normed = norm_ref[i]

        def part(f):
            w = w_ref[0, f] if first_module else w_ref[f]
            return lax.dot_general(normed, w, (((1,), (1,)), ((), ())), preferred_element_type=jnp.float32)

        q_ref[i] = (part(0) * (DH**-0.5 * LOG2E)).astype(jnp.bfloat16)
        k_ref[i] = part(1).astype(jnp.bfloat16)
        v_ref[i] = part(2).astype(jnp.bfloat16)
        g_ref[i] = jax.nn.sigmoid(part(3))

    def view(part, marks, half=None, split=None):
        first, width = gather_parts(n)[part]
        index = [me["c"]]
        for axis in "yxz":
            mark = marks[axis]
            if axis == split:
                index.append(pl.ds(2 * half, 2))
            elif mark is None:
                index.append(slice(None))
            else:
                index.append(mark)
        lines = pl.ds(16 * half, 16) if half is not None and split is None else slice(None)
        return gat_ref.at[(*index, lines, pl.ds(first, width))]

    def share(part, number, marks):
        area = view(part, marks)
        return push(area, area, shifted(me, "c", 1), (core_send, core_recv), part * 4 + number)

    def unfold(part, core, marks):
        first, width = gather_parts(n)[part]
        free = [axis for axis in "yxz" if marks[axis] is None]

        def one(t, carry):
            at = {**marks, free[0]: t // RING, free[1]: lax.rem(t, RING), "c": core}
            piece = gat_ref[core, at["y"], at["x"], at["z"], :, first:first + width].astype(jnp.float32)
            piece = jnp.where(valid[:, first:first + width], piece * LOG2E, -1e9)
            line = pl.multiple_of(block_of(at) * rows, rows)
            for h in range(HEADS):
                bias_ref[h, pl.ds(line, rows), first:first + width] = piece[h * rows:(h + 1) * rows]
            return carry

        lax.fori_loop(0, RING * RING, one, 0)

    sibling = shifted(me, "c", 1)["c"]
    pending = {}
    shared = {}
    sets = {}
    for phase in range(3):
        marks = {}
        for part, order in enumerate(ORDERS):
            axis = order[phase]
            marks[part] = {a: (None if a in order[:phase] else me[a]) for a in "yxz"}
            if phase > 0:
                for copy in pending[part]:
                    copy.wait_recv()
            area = view(part, marks[part])
            pending[part] = [
                push(area, area, shifted(me, axis, by), (send, recv), ((part * 3 + phase) * 2) * 2 + way)
                for way, by in enumerate((1, -1))
            ]
            if phase == 2:
                shared[part, 0] = share(part, 0, marks[part])
                sets[part, 0] = marks[part]
        if phase == 2:
            if first_module:
                keep_w.wait()
                w_copy.wait_recv()
            for i in range(4):
                project(i)
            for part in range(3):
                unfold(part, me["c"], sets[part, 0])
        for part, order in enumerate(ORDERS):
            axis = order[phase]
            split = order[0] if phase > 0 else None
            back = {**marks[part], axis: shifted(me, axis, -1)[axis]}
            ahead = {**marks[part], axis: shifted(me, axis, 1)[axis]}
            later_copies = []
            for way, (by, held) in enumerate(((1, back), (-1, ahead))):
                pending[part][way].wait_recv()
                area = view(part, held, half=way, split=split)
                later_copies.append(
                    push(area, area, shifted(me, axis, by), (send, recv), ((part * 3 + phase) * 2 + 1) * 2 + way)
                )
            if phase == 2:
                for number, held in ((1, back), (2, ahead)):
                    shared[part, number] = share(part, number, held)
                    sets[part, number] = held
            pending[part] = later_copies
    for i in range(4, rows):
        project(i)
    for part in range(3):
        for number in (1, 2):
            unfold(part, me["c"], sets[part, number])
        shared[part, 0].wait_recv()
        unfold(part, sibling, sets[part, 0])
    for h in range(HEADS):
        va_ref[h, :, W:] = jnp.broadcast_to((lane == h).astype(jnp.bfloat16), (n, W))
    for part, order in enumerate(ORDERS):
        for copy in pending[part]:
            copy.wait_recv()
        axis = order[2]
        sets[part, 3] = {**{a: None for a in "yxz"}, axis: shifted(me, axis, 2)[axis]}
        shared[part, 3] = share(part, 3, sets[part, 3])
    for part in range(3):
        unfold(part, me["c"], sets[part, 3])
        for number in (1, 2):
            shared[part, number].wait_recv()
            unfold(part, sibling, sets[part, number])
    for part in range(3):
        shared[part, 3].wait_recv()
        unfold(part, sibling, sets[part, 3])
    for copy in started:
        copy.wait_send()
    if first_module:
        give_w = pltpu.make_async_copy(w_ref.at[1], w_out, local_sem.at[0])
        give_w.start()

    units = [(off, h) for off in (0, span) for h in range(HEADS)]
    tiles = [(first, min(256, n - first)) for first in range(0, n, 256)]
    grains = span // 16
    cuts = [16 * (grains * t // len(tiles)) for t in range(len(tiles) + 1)]

    def row_copies(row):
        slot = rep * rows + row
        remote = pltpu.make_async_remote_copy(
            src_ref=stage_ref.at[row], dst_ref=out_ref.at[slot], send_sem=row_send.at[row], recv_sem=row_recv.at[row],
            device_id=device_of(peer), device_id_type=MESH,
        )
        return remote, pltpu.make_async_copy(stage_ref.at[row], out_ref.at[slot], row_local.at[row])

    def one_row(row, i):
        inside = (row0 + row).astype(jnp.float32) < length
        v = v_ref[row]
        for h in range(HEADS):
            va_ref[h, :, :W] = jnp.where(lane == h, v, jnp.zeros_like(v))

        def score(unit, t):
            off, h = units[unit]
            first, width = tiles[t]
            queries = q_ref[row, off:off + span, :]
            own = jnp.where(lane == h, queries, jnp.zeros_like(queries))
            score_ref[unit % 2, :, first:first + width] = lax.dot_general(
                own, k_ref[row, first:first + width, :], (((1,), (1,)), ((), ())), preferred_element_type=jnp.float32
            )

        def soften(unit, t):
            off, h = units[unit]
            for lo in range(cuts[t], cuts[t + 1], GRAIN):
                hi = min(lo + GRAIN, cuts[t + 1])
                scores = score_ref[unit % 2, lo:hi, :] + bias_ref[h, off + lo:off + hi, :]
                highest = jnp.max(scores, axis=-1, keepdims=True)
                expo_ref[unit % 2, lo:hi, :] = jnp.exp2(scores - highest).astype(jnp.bfloat16)

        def combine(unit, t):
            h = units[unit][1]
            first, width = tiles[t]
            part = jnp.dot(
                expo_ref[unit % 2, :, first:first + width], va_ref[h, first:first + width, :],
                preferred_element_type=jnp.float32,
            )
            if h == 0 and t == 0:
                total_ref[...] = part
            else:
                total_ref[...] += part

        def finish(off):
            gated = total_ref[:, :W] / total_ref[:, W:] * g_ref[row, off:off + span, :]
            update = jnp.dot(gated.astype(jnp.bfloat16), outw_ref[...], preferred_element_type=jnp.float32)
            base = base_ref[row, off:off + span, :].astype(jnp.float32)
            number = (off + lax.broadcasted_iota(jnp.int32, (span, 1), 0)).astype(jnp.float32)
            result = jnp.where((number < length) & inside, base + update, base)
            if first_module:
                done_ref[i, off:off + span, :] = result
            else:
                stage_ref[row, off:off + span, :] = result.astype(jnp.bfloat16)

        for stage in range(len(units) + 2):
            for t in range(len(tiles)):
                if stage < len(units):
                    score(stage, t)
                if stage >= 2:
                    combine(stage - 2, t)
                if 1 <= stage <= len(units):
                    soften(stage - 1, t)
            if stage >= 2 and units[stage - 2][1] == HEADS - 1:
                finish(units[stage - 2][0])

    if not first_module:
        def each_row(row, carry):
            one_row(row, None)
            for copy in row_copies(row):
                copy.start()
            return carry

        lax.fori_loop(0, rows, each_row, 0)
        for row in range(rows):
            remote, keep = row_copies(row)
            remote.wait()
            keep.wait()
        return

    mine_yc = lax.rem(me["y"], 2) * 4 + me["c"] * 2 + me["y"] // 2
    mine_xz = me["x"] * RING + me["z"]

    def first_copy(p, k):
        at = column[k]
        source = stage_ref.at[p, lax.rem(at["y"], 2), :, at["c"] * 2 + at["y"] // 2]
        goal = mail_ref.at[p, mine_yc]
        if k == 0:
            return pltpu.make_async_copy(source, goal, row_local.at[p])
        number = p * CORES * RING + k
        return pltpu.make_async_remote_copy(
            src_ref=source, dst_ref=goal, send_sem=row_send.at[number], recv_sem=row_recv.at[number],
            device_id=device_of(at), device_id_type=MESH,
        )

    def second_copy(p, k):
        at = level[k]
        source = mail_ref.at[p, :, at["x"] * RING + at["z"]]
        goal = out_ref.at[p, mine_xz]
        if k == 0:
            return pltpu.make_async_copy(source, goal, far_local.at[p])
        number = p * RING * RING + k
        return pltpu.make_async_remote_copy(
            src_ref=source, dst_ref=goal, send_sem=far_send.at[number], recv_sem=far_recv.at[number],
            device_id=device_of(at), device_id_type=MESH,
        )

    def pass_on(p):
        first_copy(p, 0).wait()
        for k in range(1, CORES * RING):
            first_copy(p, k).wait_recv()
        for k in range(RING * RING):
            second_copy(p, k).start()

    def each_pair(pair, carry):
        def one(i, inner):
            one_row(pair * 2 + i, i)
            return inner

        lax.fori_loop(0, 2, one, 0)
        both = [done_ref[i].reshape(n // rows, rows, -1) for i in range(2)]
        stage_ref[pair] = jnp.concatenate(both, axis=1).astype(jnp.bfloat16).reshape(stage_ref.shape[1:])
        for k in range(CORES * RING):
            first_copy(pair, k).start()

        @pl.when(pair > 0)
        def _():
            pass_on(pair - 1)

        return carry

    lax.fori_loop(0, steps, each_pair, 0)
    pass_on(steps - 1)
    for p in range(steps):
        for k in range(1, CORES * RING):
            first_copy(p, k).wait_send()
        second_copy(p, 0).wait()
        for k in range(1, RING * RING):
            second_copy(p, k).wait_send()
            second_copy(p, k).wait_recv()
    give_w.wait()


def module(source, mask, gain, w, bw, outw, *, first_module, n, rows, ident):
    c = source.shape[-1]
    steps = rows // 2
    yc, xz = CORES * RING, RING * RING
    shape = (rows, n, W)
    span = n // 2
    dma = pltpu.SemaphoreType.DMA
    scratch = [
        pltpu.VMEM((CORES, RING, RING, RING, HEADS * rows, n), jnp.bfloat16),
        pltpu.VMEM((HEADS, n, n), jnp.float32),
        pltpu.VMEM((rows, n, c), jnp.bfloat16),
        pltpu.VMEM(shape, jnp.bfloat16),
        pltpu.VMEM(shape, jnp.bfloat16),
        pltpu.VMEM(shape, jnp.bfloat16),
        pltpu.VMEM(shape, jnp.float32),
        pltpu.VMEM((HEADS, n, 2 * W), jnp.bfloat16),
        pltpu.VMEM((2, span, n), jnp.float32),
        pltpu.VMEM((2, span, n), jnp.bfloat16),
        pltpu.VMEM((span, 2 * W), jnp.float32),
        pltpu.VMEM((rows, n, c), jnp.bfloat16),
        pltpu.VMEM((HEADS * rows, n), jnp.float32),
        pltpu.VMEM((steps, 2, xz, yc // 2, 2 * rows, c) if first_module else (rows, n, c), jnp.bfloat16),
        dma((12,)), dma((12,)), dma((36,)), dma((36,)), dma((2,)),
    ]
    vmem = pl.BlockSpec(memory_space=pltpu.VMEM)
    hbm = pl.BlockSpec(memory_space=pl.ANY)
    if first_module:
        out_shape = [
            jax.ShapeDtypeStruct((steps, xz, yc, 2 * rows, c), jnp.bfloat16),
            jax.ShapeDtypeStruct((4, W, c), jnp.bfloat16),
            jax.ShapeDtypeStruct(bw.shape[1:], jnp.bfloat16),
        ]
        out_specs = [hbm, hbm, vmem]
        scratch += [
            dma((steps * yc,)), dma((steps * yc,)), dma((steps,)),
            pltpu.VMEM((2, n, c), jnp.float32),
            pltpu.VMEM((steps, yc, xz, 2 * rows, c), jnp.bfloat16),
            dma((steps * xz,)), dma((steps * xz,)), dma((steps,)),
            pltpu.VMEM((2, 4, W, c), jnp.bfloat16),
            pltpu.VMEM(bw.shape, jnp.bfloat16),
            dma((2,)), dma((2,)),
        ]
    else:
        out_shape = jax.ShapeDtypeStruct((2 * rows, n, c), jnp.bfloat16)
        out_specs = hbm
        scratch += [dma((rows,)), dma((rows,)), dma((rows,))]
    return pl.pallas_call(
        functools.partial(module_kernel, first_module=first_module, n=n, rows=rows),
        out_shape=out_shape,
        in_specs=[hbm if first_module else vmem] + [vmem] * 5,
        out_specs=out_specs,
        scratch_shapes=scratch,
        compiler_params=pltpu.CompilerParams(
            collective_id=ident, has_side_effects=True, vmem_limit_bytes=VMEM_LIMIT
        ),
    )(source, mask, gain, w, bw, outw)


def on_device(pair_map, residue_mask, gain_start, proj_start, bias_start, out_start, gain_end, proj_end, bias_end, out_end):
    n = pair_map.shape[1]
    rows = pair_map.shape[0] // 2
    rep = lax.axis_index("rep")
    mask = residue_mask[None, :]
    half = jnp.transpose(jnp.stack([proj_start, proj_end]), (0, 1, 3, 2))
    strip = jnp.transpose(jnp.stack([bias_start, bias_end]), (0, 2, 1))
    strip = lax.dynamic_update_slice_in_dim(
        jnp.zeros((2, 16, strip.shape[2]), strip.dtype), strip, rep * strip.shape[1], 1
    )
    inbox, w_end, strip_end = module(
        pair_map, mask, gain_start[None, :], half, strip, out_start, first_module=True, n=n, rows=rows, ident=0
    )
    return module(
        inbox, mask, gain_end[None, :], w_end, strip_end, out_end, first_module=False, n=n, rows=rows, ident=1
    )


def solution(mesh):
    in_specs = (
        P("dap", None, None), P(), P(), P(None, None, "rep"), P(None, "rep"), P(),
        P(), P(None, None, "rep"), P(None, "rep"), P(),
    )
    return jax.shard_map(on_device, mesh=mesh, in_specs=in_specs, out_specs=P("dap", None, None), check_vma=False)
```

profile of v0, /device:TPU:1, one launch (start us, length us, event | category | flops | bytes accessed | tf_op | source)
XLA Modules:
  0.0 233.1 jit_solution(9232344220423203339)
XLA Ops:
  0.0 0.7 fusion.refs_4_
  0.7 0.0 copy-start
  0.7 1.5 maximum_bitcast_fusion.refs_3_
  2.2 0.0 copy-done
  2.2 123.7 %shard_map.100 = (bf16[4,16,8,16,128]{4,3,2,1,0:T(8,128)(2,1)}, bf16[4,128,128]{2,1,0:T(8,128)(2,1)}, bf16[16,128]{1,0:T(8,128)(2,1)}) custom-call(bf16[16,1024,128]{2,1,0:T(8,128)(2,1)} %refs_0_.1, s32[1,1024]{1,0:T(1,128)} %bitcast.15, f32[1,128]{1,0:T(1,128)} %bitcast.20, bf16[2,4,64,128]{3,2,1,0:T(8,128)(2,1)} %maximum_bitcast_fusion.refs_3_, ...), custom_call_target="tpu_custom_call" | custom-call | tf_op jit(solution)/shard_map/pallas_call | solution.py:465
  126.0 102.5 %shard_map.101 = bf16[16,1024,128]{2,1,0:T(8,128)(2,1)} custom-call(bf16[4,16,8,16,128]{4,3,2,1,0:T(8,128)(2,1)} %get-tuple-element.8.refs_0_, s32[1,1024]{1,0:T(1,128)} %bitcast.16, f32[1,128]{1,0:T(1,128)} %bitcast.17, bf16[4,128,128]{2,1,0:T(8,128)(2,1)} %get-tuple-element.9.refs_3_, bf16[16,128]{1,0:T(8,128)(2,1)} %get-tuple-element.10.refs_4_, ...), custom_call_target="tpu_custom_call" | custom-call | tf_op jit(solution)/shard_map/pallas_call | solution.py:465
  228.5 4.6 %copy.13 = bf16[16,1024,128]{2,1,0:T(8,128)(2,1)} copy(bf16[16,1024,128]{2,1,0:T(8,128)(2,1)} %shard_map.101) | data formatting | bytes 8388608
  (1 shorter events, 0.0 us)
Async XLA Ops:
  0.7 1.5 copy-start
where the time goes:
time: 234 us; the launch traced here: 233 us
  Pallas kernels  226 us (97%)
  local copies, waits for them, and re-layouts  4.61 us (2%)
    pallas_call x2, Pallas kernels, module(): pl.pallas_call(functools.partial(module_kernel, first_module=first_module...  226 us

commit v1 on v0

--- a/solution.py
+++ b/solution.py
@@ -51,7 +51,8 @@
 
 
 ORDERS = ("xyz", "yzx", "zxy")
-GRAIN = 32
+GRAIN = 64
+TILES = 2
 
 
 def gather_parts(n):
@@ -62,12 +63,12 @@
 def module_kernel(*refs, first_module, n, rows):
     if first_module:
         (map_ref, mask_ref, gain_ref, half_ref, strip_ref, outw_ref, out_ref, w_out, bw_out) = refs[:9]
-        (gat_ref, bias_ref, norm_ref, q_ref, k_ref, v_ref, g_ref, va_ref, score_ref, expo_ref, total_ref, base_ref,
+        (gat_ref, bias_ref, norm_ref, q_ref, k_ref, v_ref, g_ref, vt_ref, score_ref, expo_ref, head_ref, top_ref, base_ref,
          own32, stage_ref, core_send, core_recv, send, recv, local_sem, row_send, row_recv, row_local,
          done_ref, mail_ref, far_send, far_recv, far_local, w_ref, strip_in, w_send, w_recv) = refs[9:]
     else:
         (map_ref, mask_ref, gain_ref, w_ref, bw_ref, outw_ref, out_ref) = refs[:7]
-        (gat_ref, bias_ref, norm_ref, q_ref, k_ref, v_ref, g_ref, va_ref, score_ref, expo_ref, total_ref, base_ref,
+        (gat_ref, bias_ref, norm_ref, q_ref, k_ref, v_ref, g_ref, vt_ref, score_ref, expo_ref, head_ref, top_ref, base_ref,
          own32, stage_ref, core_send, core_recv, send, recv, local_sem, row_send, row_recv, row_local) = refs[7:]
     me = place()
     rep = lax.axis_index("rep")
@@ -79,7 +80,7 @@
               for k in range(CORES * RING)]
     level = [{**me, "x": lax.rem(me["x"] + k // RING, RING), "z": lax.rem(me["z"] + k % RING, RING)}
              for k in range(RING * RING)]
-    lane = lax.broadcasted_iota(jnp.int32, (1, W), 1) // DH
+    owner = lax.broadcasted_iota(jnp.int32, (W, 1), 0) // DH
     mask = mask_ref[...].astype(jnp.float32)
     length = jnp.sum(mask, axis=1, keepdims=True)
     valid = mask > 0.5
@@ -152,15 +153,14 @@
 
     def project(i):
         normed = norm_ref[i]
-
-        def part(f):
-            w = w_ref[0, f] if first_module else w_ref[f]
-            return lax.dot_general(normed, w, (((1,), (1,)), ((), ())), preferred_element_type=jnp.float32)
-
-        q_ref[i] = (part(0) * (DH**-0.5 * LOG2E)).astype(jnp.bfloat16)
-        k_ref[i] = part(1).astype(jnp.bfloat16)
-        v_ref[i] = part(2).astype(jnp.bfloat16)
-        g_ref[i] = jax.nn.sigmoid(part(3))
+        across = (w_ref[0, :3] if first_module else w_ref[:3]).reshape(3 * W, -1)
+        down = w_ref[0, 3] if first_module else w_ref[3]
+        both = (((1,), (1,)), ((), ()))
+        turned = lax.dot_general(across, normed, both, preferred_element_type=jnp.float32)
+        q_ref[i] = (turned[:W] * (DH**-0.5 * LOG2E)).astype(jnp.bfloat16)
+        v_ref[i] = turned[W:2 * W].astype(jnp.bfloat16)
+        g_ref[i] = jax.nn.sigmoid(turned[2 * W:])
+        k_ref[i] = lax.dot_general(normed, down, both, preferred_element_type=jnp.float32).astype(jnp.bfloat16)
 
     def view(part, marks, half=None, split=None):
         first, width = gather_parts(n)[part]
@@ -247,8 +247,7 @@
             unfold(part, me["c"], sets[part, number])
         shared[part, 0].wait_recv()
         unfold(part, sibling, sets[part, 0])
-    for h in range(HEADS):
-        va_ref[h, :, W:] = jnp.broadcast_to((lane == h).astype(jnp.bfloat16), (n, W))
+    vt_ref[:, DH:, :] = jnp.ones((HEADS, 16, n), jnp.bfloat16)
     for part, order in enumerate(ORDERS):
         for copy in pending[part]:
             copy.wait_recv()
@@ -269,57 +268,66 @@
         give_w = pltpu.make_async_copy(w_ref.at[1], w_out, local_sem.at[0])
         give_w.start()
 
+    def flip(h, carry):
+        side = 128
+        for a in range(n // side):
+            for b in range(a, n // side):
+                rows_a, rows_b = slice(a * side, (a + 1) * side), slice(b * side, (b + 1) * side)
+                upper = bias_ref[h, rows_a, rows_b]
+                if a < b:
+                    lower = bias_ref[h, rows_b, rows_a]
+                    bias_ref[h, rows_a, rows_b] = lower.T
+                bias_ref[h, rows_b, rows_a] = upper.T
+        return carry
+
+    lax.fori_loop(0, HEADS, flip, 0)
+
     units = [(off, h) for off in (0, span) for h in range(HEADS)]
-    tiles = [(first, min(256, n - first)) for first in range(0, n, 256)]
-    grains = span // 16
-    cuts = [16 * (grains * t // len(tiles)) for t in range(len(tiles) + 1)]
-
-    def row_copies(row):
-        slot = rep * rows + row
+    tile = n // TILES
+
+    def row_copies(row, off):
+        source = stage_ref.at[row, pl.ds(off, span)]
+        goal = out_ref.at[rep * rows + row, pl.ds(off, span)]
+        number = row * 2 + off // span
         remote = pltpu.make_async_remote_copy(
-            src_ref=stage_ref.at[row], dst_ref=out_ref.at[slot], send_sem=row_send.at[row], recv_sem=row_recv.at[row],
+            src_ref=source, dst_ref=goal, send_sem=row_send.at[number], recv_sem=row_recv.at[number],
             device_id=device_of(peer), device_id_type=MESH,
         )
-        return remote, pltpu.make_async_copy(stage_ref.at[row], out_ref.at[slot], row_local.at[row])
+        return remote, pltpu.make_async_copy(source, goal, row_local.at[number])
 
     def one_row(row, i):
         inside = (row0 + row).astype(jnp.float32) < length
-        v = v_ref[row]
         for h in range(HEADS):
-            va_ref[h, :, :W] = jnp.where(lane == h, v, jnp.zeros_like(v))
+            vt_ref[h, :DH, :] = v_ref[row, h * DH:(h + 1) * DH, :]
 
         def score(unit, t):
             off, h = units[unit]
-            first, width = tiles[t]
-            queries = q_ref[row, off:off + span, :]
-            own = jnp.where(lane == h, queries, jnp.zeros_like(queries))
-            score_ref[unit % 2, :, first:first + width] = lax.dot_general(
-                own, k_ref[row, first:first + width, :], (((1,), (1,)), ((), ())), preferred_element_type=jnp.float32
-            )
+            keys = slice(t * tile, (t + 1) * tile)
+            queries = q_ref[row, :, off:off + span]
+            own = jnp.where(owner == h, queries, jnp.zeros_like(queries))
+            scores = jnp.dot(k_ref[row, keys, :], own, preferred_element_type=jnp.float32)
+            scores = scores + bias_ref[h, keys, off:off + span]
+            top = jnp.max(scores, axis=0, keepdims=True)
+            top_ref[unit % 2] = top if t == 0 else jnp.maximum(top, top_ref[unit % 2])
+            score_ref[unit % 2, keys, :] = scores
 
         def soften(unit, t):
-            off, h = units[unit]
-            for lo in range(cuts[t], cuts[t + 1], GRAIN):
-                hi = min(lo + GRAIN, cuts[t + 1])
-                scores = score_ref[unit % 2, lo:hi, :] + bias_ref[h, off + lo:off + hi, :]
-                highest = jnp.max(scores, axis=-1, keepdims=True)
-                expo_ref[unit % 2, lo:hi, :] = jnp.exp2(scores - highest).astype(jnp.bfloat16)
+            for first in range(t * tile, (t + 1) * tile, GRAIN):
+                keys = slice(first, first + GRAIN)
+                expo = jnp.exp2(score_ref[unit % 2, keys, :] - top_ref[unit % 2])
+                expo_ref[unit % 2, keys, :] = expo.astype(jnp.bfloat16)
 
         def combine(unit, t):
             h = units[unit][1]
-            first, width = tiles[t]
-            part = jnp.dot(
-                expo_ref[unit % 2, :, first:first + width], va_ref[h, first:first + width, :],
-                preferred_element_type=jnp.float32,
+            some = slice(t * (span // TILES), (t + 1) * (span // TILES))
+            result = jnp.dot(vt_ref[h], expo_ref[unit % 2, :, some], preferred_element_type=jnp.float32)
+            head_ref[h * DH:(h + 1) * DH, some] = result[:DH] / result[DH:DH + 1]
+
+        def finish(off):
+            gated = (head_ref[...] * g_ref[row, :, off:off + span]).astype(jnp.bfloat16)
+            update = lax.dot_general(
+                gated, outw_ref[...], (((0,), (0,)), ((), ())), preferred_element_type=jnp.float32
             )
-            if h == 0 and t == 0:
-                total_ref[...] = part
-            else:
-                total_ref[...] += part
-
-        def finish(off):
-            gated = total_ref[:, :W] / total_ref[:, W:] * g_ref[row, off:off + span, :]
-            update = jnp.dot(gated.astype(jnp.bfloat16), outw_ref[...], preferred_element_type=jnp.float32)
             base = base_ref[row, off:off + span, :].astype(jnp.float32)
             number = (off + lax.broadcasted_iota(jnp.int32, (span, 1), 0)).astype(jnp.float32)
             result = jnp.where((number < length) & inside, base + update, base)
@@ -327,9 +335,11 @@
                 done_ref[i, off:off + span, :] = result
             else:
                 stage_ref[row, off:off + span, :] = result.astype(jnp.bfloat16)
+                for copy in row_copies(row, off):
+                    copy.start()
 
         for stage in range(len(units) + 2):
-            for t in range(len(tiles)):
+            for t in range(TILES):
                 if stage < len(units):
                     score(stage, t)
                 if stage >= 2:
@@ -342,15 +352,14 @@
     if not first_module:
         def each_row(row, carry):
             one_row(row, None)
-            for copy in row_copies(row):
-                copy.start()
             return carry
 
         lax.fori_loop(0, rows, each_row, 0)
         for row in range(rows):
-            remote, keep = row_copies(row)
-            remote.wait()
-            keep.wait()
+            for off in (0, span):
+                remote, keep = row_copies(row, off)
+                remote.wait()
+                keep.wait()
         return
 
     mine_yc = lax.rem(me["y"], 2) * 4 + me["c"] * 2 + me["y"] // 2
@@ -420,21 +429,21 @@
     c = source.shape[-1]
     steps = rows // 2
     yc, xz = CORES * RING, RING * RING
-    shape = (rows, n, W)
     span = n // 2
     dma = pltpu.SemaphoreType.DMA
     scratch = [
         pltpu.VMEM((CORES, RING, RING, RING, HEADS * rows, n), jnp.bfloat16),
         pltpu.VMEM((HEADS, n, n), jnp.float32),
         pltpu.VMEM((rows, n, c), jnp.bfloat16),
-        pltpu.VMEM(shape, jnp.bfloat16),
-        pltpu.VMEM(shape, jnp.bfloat16),
-        pltpu.VMEM(shape, jnp.bfloat16),
-        pltpu.VMEM(shape, jnp.float32),
-        pltpu.VMEM((HEADS, n, 2 * W), jnp.bfloat16),
-        pltpu.VMEM((2, span, n), jnp.float32),
-        pltpu.VMEM((2, span, n), jnp.bfloat16),
-        pltpu.VMEM((span, 2 * W), jnp.float32),
+        pltpu.VMEM((rows, W, n), jnp.bfloat16),
+        pltpu.VMEM((rows, n, W), jnp.bfloat16),
+        pltpu.VMEM((rows, W, n), jnp.bfloat16),
+        pltpu.VMEM((rows, W, n), jnp.float32),
+        pltpu.VMEM((HEADS, DH + 16, n), jnp.bfloat16),
+        pltpu.VMEM((2, n, span), jnp.float32),
+        pltpu.VMEM((2, n, span), jnp.bfloat16),
+        pltpu.VMEM((W, span), jnp.float32),
+        pltpu.VMEM((2, 1, span), jnp.float32),
         pltpu.VMEM((rows, n, c), jnp.bfloat16),
         pltpu.VMEM((HEADS * rows, n), jnp.float32),
         pltpu.VMEM((steps, 2, xz, yc // 2, 2 * rows, c) if first_module else (rows, n, c), jnp.bfloat16),
@@ -461,7 +470,7 @@
     else:
         out_shape = jax.ShapeDtypeStruct((2 * rows, n, c), jnp.bfloat16)
         out_specs = hbm
-        scratch += [dma((rows,)), dma((rows,)), dma((rows,))]
+        scratch += [dma((2 * rows,)), dma((2 * rows,)), dma((2 * rows,))]
     return pl.pallas_call(
         functools.partial(module_kernel, first_module=first_module, n=n, rows=rows),
         out_shape=out_shape,
@@ -479,7 +488,8 @@
     rows = pair_map.shape[0] // 2
     rep = lax.axis_index("rep")
     mask = residue_mask[None, :]
-    half = jnp.transpose(jnp.stack([proj_start, proj_end]), (0, 1, 3, 2))
+    half = jnp.stack([proj[f] for proj in (proj_start, proj_end) for f in (0, 2, 3, 1)])
+    half = jnp.transpose(half.reshape(2, 4, *half.shape[1:]), (0, 1, 3, 2))
     strip = jnp.transpose(jnp.stack([bias_start, bias_end]), (0, 2, 1))
     strip = lax.dynamic_update_slice_in_dim(
         jnp.zeros((2, 16, strip.shape[2]), strip.dtype), strip, rep * strip.shape[1], 1

time: 234 us -> 215 us (0.919)
  Pallas kernels: 226 us -> 204 us
  local copies, waits for them, and re-layouts: 4.61 us -> 9.69 us
    pallas_call x2, Pallas kernels: 226 us -> 204 us  [module(): pl.pallas_call(functools.partial(module_kernel, first_module=first_module...]
    unnamed x3 -> x10, local copies, waits for them, and re-layouts: 4.61 us -> 8.96 us
where the time goes in v1:
time: 215 us; the launch traced here: 214 us
  Pallas kernels  204 us (95%)
  local copies, waits for them, and re-layouts  9.69 us (5%)
    pallas_call x2, Pallas kernels, module(): pl.pallas_call(functools.partial(module_kernel, first_module=first_module...  204 us
    unnamed x10, local copies, waits for them, and re-layouts  8.96 us

profile of v1, /device:TPU:1, one launch (start us, length us, event | category | flops | bytes accessed | tf_op | source)
XLA Modules:
  0.0 214.0 jit_solution(6050462840963146641)
XLA Ops:
  0.0 0.7 fusion.refs_4_
  0.7 0.0 copy-start.1
  0.7 0.7 slice_dynamic-update-slice_fusion.5
  1.4 0.8 slice_dynamic-update-slice_fusion.1
  2.2 0.7 slice_dynamic-update-slice_fusion.4
  2.9 0.7 slice_dynamic-update-slice_fusion.3
  3.6 0.8 slice_dynamic-update-slice_fusion
  4.4 0.7 slice_dynamic-update-slice_fusion.2
  5.1 0.0 copy-start
  5.1 0.0 copy-done.1
  5.1 0.7 copy-done
  5.8 108.4 %shard_map.100 = (bf16[4,16,8,16,128]{4,3,2,1,0:T(8,128)(2,1)}, bf16[4,128,128]{2,1,0:T(8,128)(2,1)}, bf16[16,128]{1,0:T(8,128)(2,1)}) custom-call(bf16[16,1024,128]{2,1,0:T(8,128)(2,1)} %refs_0_.1, s32[1,1024]{1,0:T(1,128)} %bitcast.13, f32[1,128]{1,0:T(1,128)} %bitcast.18, bf16[2,4,64,128]{3,2,1,0:T(8,128)(2,1)} %bitcast.12, ...), custom_call_target="tpu_custom_call" | custom-call | tf_op jit(solution)/shard_map/pallas_call | solution.py:474
  114.2 95.2 %shard_map.101 = bf16[16,1024,128]{2,1,0:T(8,128)(2,1)} custom-call(bf16[4,16,8,16,128]{4,3,2,1,0:T(8,128)(2,1)} %get-tuple-element.8.refs_0_, s32[1,1024]{1,0:T(1,128)} %bitcast.14, f32[1,128]{1,0:T(1,128)} %bitcast.15, bf16[4,128,128]{2,1,0:T(8,128)(2,1)} %get-tuple-element.9.refs_3_, bf16[16,128]{1,0:T(8,128)(2,1)} %get-tuple-element.10.refs_4_, ...), custom_call_target="tpu_custom_call" | custom-call | tf_op jit(solution)/shard_map/pallas_call | solution.py:474
  209.4 4.6 %copy.18 = bf16[16,1024,128]{2,1,0:T(8,128)(2,1)} copy(bf16[16,1024,128]{2,1,0:T(8,128)(2,1)} %shard_map.101) | data formatting | bytes 8388608
  (1 shorter events, 0.0 us)
Async XLA Ops:
  0.7 4.4 %copy-start.1 = (bf16[2,16,128]{2,1,0:T(8,128)(2,1)}, bf16[2,16,128]{2,1,0:T(8,128)(2,1)S(1)}, u32[]{:S(2)}) copy-start(bf16[2,16,128]{2,1,0:T(8,128)(2,1)S(1)} %fusion.refs_4_) | copy-start | bytes 24580
  5.1 0.7 copy-start

commit v2 on v1

--- a/solution.py
+++ b/solution.py
@@ -69,7 +69,7 @@
     else:
         (map_ref, mask_ref, gain_ref, w_ref, bw_ref, outw_ref, out_ref) = refs[:7]
         (gat_ref, bias_ref, norm_ref, q_ref, k_ref, v_ref, g_ref, vt_ref, score_ref, expo_ref, head_ref, top_ref, base_ref,
-         own32, stage_ref, core_send, core_recv, send, recv, local_sem, row_send, row_recv, row_local) = refs[7:]
+         own32, stage_ref, core_send, core_recv, send, recv, local_sem, row_send, row_recv, row_local, more_send, more_recv) = refs[7:]
     me = place()
     rep = lax.axis_index("rep")
     peer = shifted(me, "y", 2)
@@ -125,13 +125,16 @@
                 piece = map_ref[:, xz, 4 * low:4 * low + 4].reshape(four, -1)
                 result = jnp.dot(turn, piece, preferred_element_type=jnp.float32)
                 first = (low * RING * RING + xz) * 4 * rows
-                base_ref[:, first:first + 4 * rows, :] = result.reshape(rows, 4 * rows, -1).astype(jnp.bfloat16)
-
-    def norm_row(i, carry):
+                base_ref[:rows, first:first + 4 * rows, :] = result.reshape(rows, 4 * rows, -1).astype(jnp.bfloat16)
+
+        pl.semaphore_wait(barrier, len(partners))
+        more = push(base_ref.at[rows - 1], base_ref.at[rows], peer, (more_send, more_recv), 0)
+
+    def norm_row(i):
         norm_ref[i] = normalize(base_ref[i].astype(jnp.float32), gain_ref[...])
-        return carry
-
-    lax.fori_loop(0, rows, norm_row, 0)
+
+    for i in range(rows):
+        norm_row(i)
     if first_module:
         strip_copy.wait_recv()
         weights = strip_ref[0] + strip_in[0]
@@ -140,27 +143,22 @@
     else:
         weights = bw_ref[...]
 
-    def plane_row(i, carry):
+    for i in range(rows):
         strip = lax.dot_general(weights, norm_ref[i], (((1,), (1,)), ((), ())), preferred_element_type=jnp.float32)
         for h in range(HEADS):
-            own32[pl.ds(h * rows + i, 1), :] = strip[h:h + 1]
-        return carry
-
-    lax.fori_loop(0, rows, plane_row, 0)
+            own32[h * rows + i:h * rows + i + 1, :] = strip[h:h + 1]
+
     gat_ref[me["c"], me["y"], me["x"], me["z"]] = own32[...].astype(jnp.bfloat16)
-    if not first_module:
-        pl.semaphore_wait(barrier, len(partners))
-
     def project(i):
         normed = norm_ref[i]
-        across = (w_ref[0, :3] if first_module else w_ref[:3]).reshape(3 * W, -1)
-        down = w_ref[0, 3] if first_module else w_ref[3]
+        weights = w_ref[0] if first_module else w_ref[...]
         both = (((1,), (1,)), ((), ()))
-        turned = lax.dot_general(across, normed, both, preferred_element_type=jnp.float32)
-        q_ref[i] = (turned[:W] * (DH**-0.5 * LOG2E)).astype(jnp.bfloat16)
-        v_ref[i] = turned[W:2 * W].astype(jnp.bfloat16)
-        g_ref[i] = jax.nn.sigmoid(turned[2 * W:])
-        k_ref[i] = lax.dot_general(normed, down, both, preferred_element_type=jnp.float32).astype(jnp.bfloat16)
+        queries = lax.dot_general(weights[0], normed, both, preferred_element_type=jnp.float32)
+        q_ref[i] = (queries * (DH**-0.5 * LOG2E)).astype(jnp.bfloat16)
+        rest = lax.dot_general(weights[2:].reshape(2 * W, -1), normed, both, preferred_element_type=jnp.float32)
+        v_ref[i] = rest[:W].astype(jnp.bfloat16)
+        g_ref[i] = jax.nn.sigmoid(rest[W:])
+        k_ref[i] = lax.dot_general(normed, weights[1], both, preferred_element_type=jnp.float32).astype(jnp.bfloat16)
 
     def view(part, marks, half=None, split=None):
         first, width = gather_parts(n)[part]
@@ -207,11 +205,13 @@
             if phase > 0:
                 for copy in pending[part]:
                     copy.wait_recv()
-            area = view(part, marks[part])
-            pending[part] = [
-                push(area, area, shifted(me, axis, by), (send, recv), ((part * 3 + phase) * 2) * 2 + way)
-                for way, by in enumerate((1, -1))
-            ]
+            split = order[0] if phase > 0 else None
+            pending[part] = []
+            for kind in range(2):
+                for way, by in enumerate((1, -1)):
+                    area = view(part, marks[part], half=kind ^ way, split=split)
+                    number = ((part * 3 + phase) * 3 + kind) * 2 + way
+                    pending[part].append(push(area, area, shifted(me, axis, by), (send, recv), number))
             if phase == 2:
                 shared[part, 0] = share(part, 0, marks[part])
                 sets[part, 0] = marks[part]
@@ -233,15 +233,23 @@
                 pending[part][way].wait_recv()
                 area = view(part, held, half=way, split=split)
                 later_copies.append(
-                    push(area, area, shifted(me, axis, by), (send, recv), ((part * 3 + phase) * 2 + 1) * 2 + way)
+                    push(area, area, shifted(me, axis, by), (send, recv), ((part * 3 + phase) * 3 + 2) * 2 + way)
                 )
-            if phase == 2:
-                for number, held in ((1, back), (2, ahead)):
-                    shared[part, number] = share(part, number, held)
-                    sets[part, number] = held
-            pending[part] = later_copies
+            sets[part, 1], sets[part, 2] = back, ahead
+            pending[part] = pending[part][2:] + later_copies
+        if phase == 2:
+            for part in range(3):
+                for copy in pending[part][:2]:
+                    copy.wait_recv()
+                pending[part] = pending[part][2:]
+                for number in (1, 2):
+                    shared[part, number] = share(part, number, sets[part, number])
     for i in range(4, rows):
         project(i)
+    if not first_module:
+        more.wait_recv()
+        norm_row(rows)
+        project(rows)
     for part in range(3):
         for number in (1, 2):
             unfold(part, me["c"], sets[part, number])
@@ -285,18 +293,26 @@
     units = [(off, h) for off in (0, span) for h in range(HEADS)]
     tile = n // TILES
 
-    def row_copies(row, off):
-        source = stage_ref.at[row, pl.ds(off, span)]
-        goal = out_ref.at[rep * rows + row, pl.ds(off, span)]
+    def away(row):
+        return (row // rows) * ((1 - 2 * rep) * rows - 1)
+
+    def row_ends(row, off):
+        return stage_ref.at[row, pl.ds(off, span)], out_ref.at[rep * rows + row + away(row), pl.ds(off, span)]
+
+    def row_keep(row, off):
+        source, goal = row_ends(row, off)
+        return pltpu.make_async_copy(source, goal, row_local.at[row * 2 + off // span])
+
+    def row_give(row, off):
+        source, goal = row_ends(row, off)
         number = row * 2 + off // span
-        remote = pltpu.make_async_remote_copy(
+        return pltpu.make_async_remote_copy(
             src_ref=source, dst_ref=goal, send_sem=row_send.at[number], recv_sem=row_recv.at[number],
             device_id=device_of(peer), device_id_type=MESH,
         )
-        return remote, pltpu.make_async_copy(source, goal, row_local.at[number])
 
     def one_row(row, i):
-        inside = (row0 + row).astype(jnp.float32) < length
+        inside = (row0 + row + away(row)).astype(jnp.float32) < length
         for h in range(HEADS):
             vt_ref[h, :DH, :] = v_ref[row, h * DH:(h + 1) * DH, :]
 
@@ -335,8 +351,11 @@
                 done_ref[i, off:off + span, :] = result
             else:
                 stage_ref[row, off:off + span, :] = result.astype(jnp.bfloat16)
-                for copy in row_copies(row, off):
-                    copy.start()
+                row_keep(row, off).start()
+
+                @pl.when(row < rows - 1)
+                def _():
+                    row_give(row, off).start()
 
         for stage in range(len(units) + 2):
             for t in range(TILES):
@@ -354,12 +373,12 @@
             one_row(row, None)
             return carry
 
-        lax.fori_loop(0, rows, each_row, 0)
-        for row in range(rows):
+        lax.fori_loop(0, rows + 1, each_row, 0)
+        for row in range(rows + 1):
             for off in (0, span):
-                remote, keep = row_copies(row, off)
-                remote.wait()
-                keep.wait()
+                row_keep(row, off).wait()
+                if row < rows - 1:
+                    row_give(row, off).wait()
         return
 
     mine_yc = lax.rem(me["y"], 2) * 4 + me["c"] * 2 + me["y"] // 2
@@ -430,24 +449,25 @@
     steps = rows // 2
     yc, xz = CORES * RING, RING * RING
     span = n // 2
+    held = rows if first_module else rows + 1
     dma = pltpu.SemaphoreType.DMA
     scratch = [
         pltpu.VMEM((CORES, RING, RING, RING, HEADS * rows, n), jnp.bfloat16),
         pltpu.VMEM((HEADS, n, n), jnp.float32),
-        pltpu.VMEM((rows, n, c), jnp.bfloat16),
-        pltpu.VMEM((rows, W, n), jnp.bfloat16),
-        pltpu.VMEM((rows, n, W), jnp.bfloat16),
-        pltpu.VMEM((rows, W, n), jnp.bfloat16),
-        pltpu.VMEM((rows, W, n), jnp.float32),
+        pltpu.VMEM((held, n, c), jnp.bfloat16),
+        pltpu.VMEM((held, W, n), jnp.bfloat16),
+        pltpu.VMEM((held, n, W), jnp.bfloat16),
+        pltpu.VMEM((held, W, n), jnp.bfloat16),
+        pltpu.VMEM((held, W, n), jnp.float32),
         pltpu.VMEM((HEADS, DH + 16, n), jnp.bfloat16),
         pltpu.VMEM((2, n, span), jnp.float32),
         pltpu.VMEM((2, n, span), jnp.bfloat16),
         pltpu.VMEM((W, span), jnp.float32),
         pltpu.VMEM((2, 1, span), jnp.float32),
-        pltpu.VMEM((rows, n, c), jnp.bfloat16),
+        pltpu.VMEM((held, n, c), jnp.bfloat16),
         pltpu.VMEM((HEADS * rows, n), jnp.float32),
-        pltpu.VMEM((steps, 2, xz, yc // 2, 2 * rows, c) if first_module else (rows, n, c), jnp.bfloat16),
-        dma((12,)), dma((12,)), dma((36,)), dma((36,)), dma((2,)),
+        pltpu.VMEM((steps, 2, xz, yc // 2, 2 * rows, c) if first_module else (held, n, c), jnp.bfloat16),
+        dma((12,)), dma((12,)), dma((54,)), dma((54,)), dma((2,)),
     ]
     vmem = pl.BlockSpec(memory_space=pltpu.VMEM)
     hbm = pl.BlockSpec(memory_space=pl.ANY)
@@ -470,7 +490,7 @@
     else:
         out_shape = jax.ShapeDtypeStruct((2 * rows, n, c), jnp.bfloat16)
         out_specs = hbm
-        scratch += [dma((2 * rows,)), dma((2 * rows,)), dma((2 * rows,))]
+        scratch += [dma((2 * held,)), dma((2 * held,)), dma((2 * held,)), dma((1,)), dma((1,))]
     return pl.pallas_call(
         functools.partial(module_kernel, first_module=first_module, n=n, rows=rows),
         out_shape=out_shape,
@@ -488,8 +508,7 @@
     rows = pair_map.shape[0] // 2
     rep = lax.axis_index("rep")
     mask = residue_mask[None, :]
-    half = jnp.stack([proj[f] for proj in (proj_start, proj_end) for f in (0, 2, 3, 1)])
-    half = jnp.transpose(half.reshape(2, 4, *half.shape[1:]), (0, 1, 3, 2))
+    half = jnp.transpose(jnp.stack([proj_start, proj_end]), (0, 1, 3, 2))
     strip = jnp.transpose(jnp.stack([bias_start, bias_end]), (0, 2, 1))
     strip = lax.dynamic_update_slice_in_dim(
         jnp.zeros((2, 16, strip.shape[2]), strip.dtype), strip, rep * strip.shape[1], 1

time: 215 us -> 204 us (0.949)
  Pallas kernels: 204 us -> 197 us
  local copies, waits for them, and re-layouts: 9.69 us -> 4.61 us
    pallas_call x2, Pallas kernels: 204 us -> 197 us  [module(): pl.pallas_call(functools.partial(module_kernel, first_module=first_module...]
    unnamed x10 -> x3, local copies, waits for them, and re-layouts: 8.96 us -> 4.61 us
where the time goes in v2:
time: 204 us
  Pallas kernels  197 us (97%)
  local copies, waits for them, and re-layouts  4.61 us (2%)
  other arithmetic  2.23 us (1%)
    pallas_call x2, Pallas kernels, module(): pl.pallas_call(functools.partial(module_kernel, first_module=first_module...  197 us
    unnamed x3, local copies, waits for them, and re-layouts  4.61 us

profile of v2, /device:TPU:1, one launch (start us, length us, event | category | flops | bytes accessed | tf_op | source)
XLA Modules:
  0.0 203.8 jit_solution(4806026778600557876)
XLA Ops:
  0.0 0.7 fusion.refs_4_
  0.7 0.0 copy-start
  0.7 1.5 maximum_bitcast_fusion.refs_3_
  2.2 0.0 copy-done
  2.2 105.8 %shard_map.100 = (bf16[4,16,8,16,128]{4,3,2,1,0:T(8,128)(2,1)}, bf16[4,128,128]{2,1,0:T(8,128)(2,1)}, bf16[16,128]{1,0:T(8,128)(2,1)}) custom-call(bf16[16,1024,128]{2,1,0:T(8,128)(2,1)} %refs_0_.1, s32[1,1024]{1,0:T(1,128)} %bitcast.15, f32[1,128]{1,0:T(1,128)} %bitcast.20, bf16[2,4,64,128]{3,2,1,0:T(8,128)(2,1)} %maximum_bitcast_fusion.refs_3_, ...), custom_call_target="tpu_custom_call" | custom-call | tf_op jit(solution)/shard_map/pallas_call | solution.py:494
  108.0 91.2 %shard_map.101 = bf16[16,1024,128]{2,1,0:T(8,128)(2,1)} custom-call(bf16[4,16,8,16,128]{4,3,2,1,0:T(8,128)(2,1)} %get-tuple-element.8.refs_0_, s32[1,1024]{1,0:T(1,128)} %bitcast.16, f32[1,128]{1,0:T(1,128)} %bitcast.17, bf16[4,128,128]{2,1,0:T(8,128)(2,1)} %get-tuple-element.9.refs_3_, bf16[16,128]{1,0:T(8,128)(2,1)} %get-tuple-element.10.refs_4_, ...), custom_call_target="tpu_custom_call" | custom-call | tf_op jit(solution)/shard_map/pallas_call | solution.py:494
  199.2 4.6 %copy.13 = bf16[16,1024,128]{2,1,0:T(8,128)(2,1)} copy(bf16[16,1024,128]{2,1,0:T(8,128)(2,1)} %shard_map.101) | data formatting | bytes 8388608
  (1 shorter events, 0.0 us)
Async XLA Ops:
  0.7 1.5 copy-start

commit v3 on v2

--- a/solution.py
+++ b/solution.py
@@ -88,7 +88,7 @@
     if first_module:
         partners = column[1:] + level[1:]
     else:
-        partners = [shifted(me, axis, by) for axis in "xyz" for by in (1, -1)] + [shifted(me, "c", 1), peer]
+        partners = [shifted(me, axis, by) for axis in "xyz" for by in (1, -1, 2)] + [shifted(me, "c", 1)]
     barrier = pltpu.get_barrier_semaphore()
     for partner in partners:
         pl.semaphore_signal(barrier, inc=1, device_id=device_of(partner), device_id_type=MESH)
@@ -205,11 +205,17 @@
             if phase > 0:
                 for copy in pending[part]:
                     copy.wait_recv()
-            split = order[0] if phase > 0 else None
             pending[part] = []
+            if phase < 2:
+                area = view(part, marks[part])
+                for number, by in enumerate((1, -1, 2)):
+                    pending[part].append(
+                        push(area, area, shifted(me, axis, by), (send, recv), (part * 3 + phase) * 6 + number)
+                    )
+                continue
             for kind in range(2):
                 for way, by in enumerate((1, -1)):
-                    area = view(part, marks[part], half=kind ^ way, split=split)
+                    area = view(part, marks[part], half=kind ^ way, split=order[0])
                     number = ((part * 3 + phase) * 3 + kind) * 2 + way
                     pending[part].append(push(area, area, shifted(me, axis, by), (send, recv), number))
             if phase == 2:
@@ -223,9 +229,11 @@
                 project(i)
             for part in range(3):
                 unfold(part, me["c"], sets[part, 0])
+        if phase < 2:
+            continue
         for part, order in enumerate(ORDERS):
             axis = order[phase]
-            split = order[0] if phase > 0 else None
+            split = order[0]
             back = {**marks[part], axis: shifted(me, axis, -1)[axis]}
             ahead = {**marks[part], axis: shifted(me, axis, 1)[axis]}
             later_copies = []
@@ -255,7 +263,7 @@
             unfold(part, me["c"], sets[part, number])
         shared[part, 0].wait_recv()
         unfold(part, sibling, sets[part, 0])
-    vt_ref[:, DH:, :] = jnp.ones((HEADS, 16, n), jnp.bfloat16)
+    vt_ref[:, :, DH:, :] = jnp.ones((*vt_ref.shape[:2], 16, n), jnp.bfloat16)
     for part, order in enumerate(ORDERS):
         for copy in pending[part]:
             copy.wait_recv()
@@ -290,7 +298,6 @@
 
     lax.fori_loop(0, HEADS, flip, 0)
 
-    units = [(off, h) for off in (0, span) for h in range(HEADS)]
     tile = n // TILES
 
     def away(row):
@@ -311,18 +318,17 @@
             device_id=device_of(peer), device_id_type=MESH,
         )
 
-    def one_row(row, i):
-        inside = (row0 + row + away(row)).astype(jnp.float32) < length
-        for h in range(HEADS):
-            vt_ref[h, :DH, :] = v_ref[row, h * DH:(h + 1) * DH, :]
+    def run(units):
+        for slot, row, _, h in units:
+            vt_ref[slot, h, :DH, :] = v_ref[row, h * DH:(h + 1) * DH, :]
 
         def score(unit, t):
-            off, h = units[unit]
+            _, row, off, h = units[unit]
             keys = slice(t * tile, (t + 1) * tile)
-            queries = q_ref[row, :, off:off + span]
+            queries = q_ref[row, :, pl.ds(off, span)]
             own = jnp.where(owner == h, queries, jnp.zeros_like(queries))
             scores = jnp.dot(k_ref[row, keys, :], own, preferred_element_type=jnp.float32)
-            scores = scores + bias_ref[h, keys, off:off + span]
+            scores = scores + bias_ref[h, keys, pl.ds(off, span)]
             top = jnp.max(scores, axis=0, keepdims=True)
             top_ref[unit % 2] = top if t == 0 else jnp.maximum(top, top_ref[unit % 2])
             score_ref[unit % 2, keys, :] = scores
@@ -334,21 +340,22 @@
                 expo_ref[unit % 2, keys, :] = expo.astype(jnp.bfloat16)
 
         def combine(unit, t):
-            h = units[unit][1]
+            slot, _, _, h = units[unit]
             some = slice(t * (span // TILES), (t + 1) * (span // TILES))
-            result = jnp.dot(vt_ref[h], expo_ref[unit % 2, :, some], preferred_element_type=jnp.float32)
+            result = jnp.dot(vt_ref[slot, h], expo_ref[unit % 2, :, some], preferred_element_type=jnp.float32)
             head_ref[h * DH:(h + 1) * DH, some] = result[:DH] / result[DH:DH + 1]
 
-        def finish(off):
-            gated = (head_ref[...] * g_ref[row, :, off:off + span]).astype(jnp.bfloat16)
+        def finish(slot, row, off, _):
+            inside = (row0 + row + away(row)).astype(jnp.float32) < length
+            gated = (head_ref[...] * g_ref[row, :, pl.ds(off, span)]).astype(jnp.bfloat16)
             update = lax.dot_general(
                 gated, outw_ref[...], (((0,), (0,)), ((), ())), preferred_element_type=jnp.float32
             )
-            base = base_ref[row, off:off + span, :].astype(jnp.float32)
+            base = base_ref[row, pl.ds(off, span), :].astype(jnp.float32)
             number = (off + lax.broadcasted_iota(jnp.int32, (span, 1), 0)).astype(jnp.float32)
             result = jnp.where((number < length) & inside, base + update, base)
             if first_module:
-                done_ref[i, off:off + span, :] = result
+                done_ref[slot] = result
             else:
                 stage_ref[row, off:off + span, :] = result.astype(jnp.bfloat16)
                 row_keep(row, off).start()
@@ -365,12 +372,12 @@
                     combine(stage - 2, t)
                 if 1 <= stage <= len(units):
                     soften(stage - 1, t)
-            if stage >= 2 and units[stage - 2][1] == HEADS - 1:
-                finish(units[stage - 2][0])
+            if stage >= 2 and units[stage - 2][3] == HEADS - 1:
+                finish(*units[stage - 2])
 
     if not first_module:
         def each_row(row, carry):
-            one_row(row, None)
+            run([(0, row, off, h) for off in (0, span) for h in range(HEADS)])
             return carry
 
         lax.fori_loop(0, rows + 1, each_row, 0)
@@ -384,13 +391,13 @@
     mine_yc = lax.rem(me["y"], 2) * 4 + me["c"] * 2 + me["y"] // 2
     mine_xz = me["x"] * RING + me["z"]
 
-    def first_copy(p, k):
-        at = column[k]
+    def first_copy(p, dy, dc):
+        at = {**me, "y": lax.rem(me["y"] + dy, RING), "c": lax.rem(me["c"] + dc, CORES)}
         source = stage_ref.at[p, lax.rem(at["y"], 2), :, at["c"] * 2 + at["y"] // 2]
         goal = mail_ref.at[p, mine_yc]
-        if k == 0:
+        if dc == 0 and isinstance(dy, int) and dy == 0:
             return pltpu.make_async_copy(source, goal, row_local.at[p])
-        number = p * CORES * RING + k
+        number = (p * RING + dy) * CORES + dc
         return pltpu.make_async_remote_copy(
             src_ref=source, dst_ref=goal, send_sem=row_send.at[number], recv_sem=row_recv.at[number],
             device_id=device_of(at), device_id_type=MESH,
@@ -409,22 +416,34 @@
         )
 
     def pass_on(p):
-        first_copy(p, 0).wait()
+        first_copy(p, 0, 0).wait()
         for k in range(1, CORES * RING):
-            first_copy(p, k).wait_recv()
+            first_copy(p, k // CORES, k % CORES).wait_recv()
         for k in range(RING * RING):
             second_copy(p, k).start()
 
     def each_pair(pair, carry):
-        def one(i, inner):
-            one_row(pair * 2 + i, i)
+        def each_span(side, inner):
+            off = pl.multiple_of(side * span, span)
+            run([(i, pair * 2 + i, off, h) for i in range(2) for h in range(HEADS)])
+            both = [done_ref[i].reshape(span // rows, rows, -1) for i in range(2)]
+            stage_ref[pair, side] = jnp.concatenate(both, axis=1).astype(jnp.bfloat16).reshape(stage_ref.shape[2:])
+            odd = lax.rem(side + me["y"], 2)
+
+            @pl.when(odd == 0)
+            def _():
+                first_copy(pair, 0, 0).start()
+
+            @pl.when(odd == 1)
+            def _():
+                first_copy(pair, 1, 0).start()
+
+            first_copy(pair, odd, 1).start()
+            first_copy(pair, odd + 2, 0).start()
+            first_copy(pair, odd + 2, 1).start()
             return inner
 
-        lax.fori_loop(0, 2, one, 0)
-        both = [done_ref[i].reshape(n // rows, rows, -1) for i in range(2)]
-        stage_ref[pair] = jnp.concatenate(both, axis=1).astype(jnp.bfloat16).reshape(stage_ref.shape[1:])
-        for k in range(CORES * RING):
-            first_copy(pair, k).start()
+        lax.fori_loop(0, 2, each_span, 0)
 
         @pl.when(pair > 0)
         def _():
@@ -436,7 +455,7 @@
     pass_on(steps - 1)
     for p in range(steps):
         for k in range(1, CORES * RING):
-            first_copy(p, k).wait_send()
+            first_copy(p, k // CORES, k % CORES).wait_send()
         second_copy(p, 0).wait()
         for k in range(1, RING * RING):
             second_copy(p, k).wait_send()
@@ -459,7 +478,7 @@
         pltpu.VMEM((held, n, W), jnp.bfloat16),
         pltpu.VMEM((held, W, n), jnp.bfloat16),
         pltpu.VMEM((held, W, n), jnp.float32),
-        pltpu.VMEM((HEADS, DH + 16, n), jnp.bfloat16),
+        pltpu.VMEM((2 if first_module else 1, HEADS, DH + 16, n), jnp.bfloat16),
         pltpu.VMEM((2, n, span), jnp.float32),
         pltpu.VMEM((2, n, span), jnp.bfloat16),
         pltpu.VMEM((W, span), jnp.float32),
@@ -480,7 +499,7 @@
         out_specs = [hbm, hbm, vmem]
         scratch += [
             dma((steps * yc,)), dma((steps * yc,)), dma((steps,)),
-            pltpu.VMEM((2, n, c), jnp.float32),
+            pltpu.VMEM((2, span, c), jnp.float32),
             pltpu.VMEM((steps, yc, xz, 2 * rows, c), jnp.bfloat16),
             dma((steps * xz,)), dma((steps * xz,)), dma((steps,)),
             pltpu.VMEM((2, 4, W, c), jnp.bfloat16),

time: 204 us -> 200 us (0.980)
  Pallas kernels: 197 us -> 192 us
    pallas_call x2, Pallas kernels: 197 us -> 192 us  [module(): pl.pallas_call(functools.partial(module_kernel, first_module=first_module...]
where the time goes in v3:
time: 200 us; the launch traced here: 199 us
  Pallas kernels  192 us (96%)
  local copies, waits for them, and re-layouts  4.61 us (2%)
  other arithmetic  2.23 us (1%)
    pallas_call x2, Pallas kernels, module(): pl.pallas_call(functools.partial(module_kernel, first_module=first_module...  192 us
    unnamed x3, local copies, waits for them, and re-layouts  4.61 us

profile of v3, /device:TPU:1, one launch (start us, length us, event | category | flops | bytes accessed | tf_op | source)
XLA Modules:
  0.0 199.3 jit_solution(1826693956177772846)
XLA Ops:
  0.0 0.7 fusion.refs_4_
  0.7 0.0 copy-start
  0.7 1.5 maximum_bitcast_fusion.refs_3_
  2.2 0.0 copy-done
  2.2 99.9 %shard_map.100 = (bf16[4,16,8,16,128]{4,3,2,1,0:T(8,128)(2,1)}, bf16[4,128,128]{2,1,0:T(8,128)(2,1)}, bf16[16,128]{1,0:T(8,128)(2,1)}) custom-call(bf16[16,1024,128]{2,1,0:T(8,128)(2,1)} %refs_0_.1, s32[1,1024]{1,0:T(1,128)} %bitcast.15, f32[1,128]{1,0:T(1,128)} %bitcast.20, bf16[2,4,64,128]{3,2,1,0:T(8,128)(2,1)} %maximum_bitcast_fusion.refs_3_, ...), custom_call_target="tpu_custom_call" | custom-call | tf_op jit(solution)/shard_map/pallas_call | solution.py:513
  102.2 92.5 %shard_map.101 = bf16[16,1024,128]{2,1,0:T(8,128)(2,1)} custom-call(bf16[4,16,8,16,128]{4,3,2,1,0:T(8,128)(2,1)} %get-tuple-element.8.refs_0_, s32[1,1024]{1,0:T(1,128)} %bitcast.16, f32[1,128]{1,0:T(1,128)} %bitcast.17, bf16[4,128,128]{2,1,0:T(8,128)(2,1)} %get-tuple-element.9.refs_3_, bf16[16,128]{1,0:T(8,128)(2,1)} %get-tuple-element.10.refs_4_, ...), custom_call_target="tpu_custom_call" | custom-call | tf_op jit(solution)/shard_map/pallas_call | solution.py:513
  194.7 4.6 %copy.13 = bf16[16,1024,128]{2,1,0:T(8,128)(2,1)} copy(bf16[16,1024,128]{2,1,0:T(8,128)(2,1)} %shard_map.101) | data formatting | bytes 8388608
  (1 shorter events, 0.0 us)
Async XLA Ops:
  0.7 1.5 copy-start

commit v4 on v3

--- a/solution.py
+++ b/solution.py
@@ -120,35 +120,38 @@
         come = lax.broadcasted_iota(jnp.int32, (four, four), 1)
         j, which, i = to // (4 * rows), (to // rows) % 4, to % rows
         turn = (come == ((i // 2 * 4 + which) * 2 + i % 2) * rows + j).astype(jnp.bfloat16)
-        for low in range(2):
-            for xz in range(RING * RING):
+        pl.semaphore_wait(barrier, len(partners))
+
+    def norm_row(i):
+        norm_ref[i] = normalize(base_ref[i].astype(jnp.float32), gain_ref[...])
+
+    def make_part(part):
+        first, width = gather_parts(n)[part]
+        here = slice(first, first + width)
+        if not first_module:
+            for group in range(first // (4 * rows), (first + width) // (4 * rows)):
+                low, xz = group // (RING * RING), group % (RING * RING)
                 piece = map_ref[:, xz, 4 * low:4 * low + 4].reshape(four, -1)
                 result = jnp.dot(turn, piece, preferred_element_type=jnp.float32)
-                first = (low * RING * RING + xz) * 4 * rows
-                base_ref[:rows, first:first + 4 * rows, :] = result.reshape(rows, 4 * rows, -1).astype(jnp.bfloat16)
-
-        pl.semaphore_wait(barrier, len(partners))
-        more = push(base_ref.at[rows - 1], base_ref.at[rows], peer, (more_send, more_recv), 0)
-
-    def norm_row(i):
-        norm_ref[i] = normalize(base_ref[i].astype(jnp.float32), gain_ref[...])
-
-    for i in range(rows):
-        norm_row(i)
-    if first_module:
-        strip_copy.wait_recv()
-        weights = strip_ref[0] + strip_in[0]
-        later = strip_ref[1] + strip_in[1]
-        bw_out[...] = later
-    else:
-        weights = bw_ref[...]
-
-    for i in range(rows):
-        strip = lax.dot_general(weights, norm_ref[i], (((1,), (1,)), ((), ())), preferred_element_type=jnp.float32)
-        for h in range(HEADS):
-            own32[h * rows + i:h * rows + i + 1, :] = strip[h:h + 1]
-
-    gat_ref[me["c"], me["y"], me["x"], me["z"]] = own32[...].astype(jnp.bfloat16)
+                base_ref[:rows, group * 4 * rows:(group + 1) * 4 * rows, :] = (
+                    result.reshape(rows, 4 * rows, -1).astype(jnp.bfloat16)
+                )
+        for i in range(rows):
+            norm_ref[i, here, :] = normalize(base_ref[i, here, :].astype(jnp.float32), gain_ref[...])
+        if first_module:
+            if part == 0:
+                strip_copy.wait_recv()
+            weights = strip_ref[0] + strip_in[0]
+        else:
+            weights = bw_ref[...]
+        for i in range(rows):
+            strip = lax.dot_general(
+                weights, norm_ref[i, here, :], (((1,), (1,)), ((), ())), preferred_element_type=jnp.float32
+            )
+            for h in range(HEADS):
+                own32[h * rows + i:h * rows + i + 1, here] = strip[h:h + 1]
+        gat_ref[me["c"], me["y"], me["x"], me["z"], :, here] = own32[:, here].astype(jnp.bfloat16)
+
     def project(i):
         normed = norm_ref[i]
         weights = w_ref[0] if first_module else w_ref[...]
@@ -206,6 +209,8 @@
                 for copy in pending[part]:
                     copy.wait_recv()
             pending[part] = []
+            if phase == 0:
+                make_part(part)
             if phase < 2:
                 area = view(part, marks[part])
                 for number, by in enumerate((1, -1, 2)):
@@ -229,6 +234,10 @@
                 project(i)
             for part in range(3):
                 unfold(part, me["c"], sets[part, 0])
+        if phase == 0 and first_module:
+            bw_out[...] = strip_ref[1] + strip_in[1]
+        elif phase == 0:
+            more = push(base_ref.at[rows - 1], base_ref.at[rows], peer, (more_send, more_recv), 0)
         if phase < 2:
             continue
         for part, order in enumerate(ORDERS):

time: 200 us -> 204 us (1.020)
  Pallas kernels: 192 us -> 197 us
    pallas_call x2, Pallas kernels: 192 us -> 197 us  [module(): pl.pallas_call(functools.partial(module_kernel, first_module=first_module...]
where the time goes in v4:
time: 204 us
  Pallas kernels  197 us (97%)
  local copies, waits for them, and re-layouts  4.61 us (2%)
  other arithmetic  2.23 us (1%)
    pallas_call x2, Pallas kernels, module(): pl.pallas_call(functools.partial(module_kernel, first_module=first_module...  197 us
    unnamed x3, local copies, waits for them, and re-layouts  4.61 us

profile of v4, /device:TPU:1, one launch (start us, length us, event | category | flops | bytes accessed | tf_op | source)
XLA Modules:
  0.0 203.9 jit_solution(11834725564533259385)
XLA Ops:
  0.0 0.7 fusion.refs_4_
  0.7 0.0 copy-start
  0.7 1.5 maximum_bitcast_fusion.refs_3_
  2.2 0.0 copy-done
  2.2 99.7 %shard_map.100 = (bf16[4,16,8,16,128]{4,3,2,1,0:T(8,128)(2,1)}, bf16[4,128,128]{2,1,0:T(8,128)(2,1)}, bf16[16,128]{1,0:T(8,128)(2,1)}) custom-call(bf16[16,1024,128]{2,1,0:T(8,128)(2,1)} %refs_0_.1, s32[1,1024]{1,0:T(1,128)} %bitcast.15, f32[1,128]{1,0:T(1,128)} %bitcast.20, bf16[2,4,64,128]{3,2,1,0:T(8,128)(2,1)} %maximum_bitcast_fusion.refs_3_, ...), custom_call_target="tpu_custom_call" | custom-call | tf_op jit(solution)/shard_map/pallas_call | solution.py:522
  101.9 97.4 %shard_map.101 = bf16[16,1024,128]{2,1,0:T(8,128)(2,1)} custom-call(bf16[4,16,8,16,128]{4,3,2,1,0:T(8,128)(2,1)} %get-tuple-element.8.refs_0_, s32[1,1024]{1,0:T(1,128)} %bitcast.16, f32[1,128]{1,0:T(1,128)} %bitcast.17, bf16[4,128,128]{2,1,0:T(8,128)(2,1)} %get-tuple-element.9.refs_3_, bf16[16,128]{1,0:T(8,128)(2,1)} %get-tuple-element.10.refs_4_, ...), custom_call_target="tpu_custom_call" | custom-call | tf_op jit(solution)/shard_map/pallas_call | solution.py:522
  199.3 4.6 %copy.13 = bf16[16,1024,128]{2,1,0:T(8,128)(2,1)} copy(bf16[16,1024,128]{2,1,0:T(8,128)(2,1)} %shard_map.101) | data formatting | bytes 8388608
  (1 shorter events, 0.0 us)
Async XLA Ops:
  0.7 1.5 copy-start
